TPU v7x, 128 devices: a whole 4x4x4 slice. The times are simulated.
128 devices in a mesh: row: 16 (over x, y_lo, core), col: 8 (over y_hi, z).
Axes of the slice: x: 4, y: 4 (y_hi: 2, y_lo: 2; y = y_hi * 2 + y_lo), z: 4, core: 2. Of those that a mesh axis runs over, the one named last changes fastest.
Arguments:
- blocks: bfloat16 [1024, 64, 128, 128], P('row', 'col'), may hold values from -0.109375 to 0.109375
- columns: int32 [1024, 64], P('row', 'col'), may hold values from 0 to 127
- counts: int32 [1024, 8], P('row', 'col'), may hold values from 1 to 8, as said below
- vectors: bfloat16 [1024, 32, 128], P(('col', 'row')), may hold values from -6 to 6
Outputs:
- first_image: bfloat16 [1024, 32, 128], P(('row', 'col'))
- first_back: bfloat16 [1024, 32, 128], P(('col', 'row'))
- second_image: bfloat16 [1024, 32, 128], P(('row', 'col'))
- second_back: bfloat16 [1024, 32, 128], P(('col', 'row'))
Inputs may be any that keep to these rules, and one draw needn't show every extreme that they name: `counts`: the live slots are the leading ones; the largest count, 8, is reached in every draw.
All inputs are finite; a program needn't handle non-finite values.
Results may differ from a plain program's by a relative error of at most 0.022.
Values may be sent and summed in bfloat16 or wider, within the bound.
A program may use at most 64 MiB of HBM per device.

v0:
```python
import jax
import jax.numpy as jnp
from jax import lax
from jax.sharding import PartitionSpec as P


def pick_blocks(column_vecs, columns, active):
    return column_vecs[columns] * active.astype(jnp.bfloat16)[:, :, None, None]


def forward_terms(blocks, picked):
    return jnp.einsum("isrc,iskc->ikr", blocks, picked, preferred_element_type=jnp.float32)


def adjoint_terms(blocks, columns, active, row_vecs, col_count):
    terms = jnp.einsum("isrc,ikr->iskc", blocks, row_vecs, preferred_element_type=jnp.float32)
    terms = terms * active.astype(jnp.float32)[:, :, None, None]
    slot_total = terms.shape[0] * terms.shape[1]
    return jax.ops.segment_sum(
        terms.reshape(slot_total, terms.shape[2], terms.shape[3]),
        columns.reshape(slot_total),
        num_segments=col_count,
    )


def body(blocks, columns, counts, vectors):
    vec_count = vectors.shape[0]
    col_count = vec_count * lax.axis_size("row")
    slot_ids = jnp.arange(columns.shape[1], dtype=jnp.int32)
    active = slot_ids[None, :] < counts
    results = []
    current = vectors
    for round_no in range(2):
        column_vecs = lax.all_gather(current, "row", axis=0, tiled=True)
        picked = pick_blocks(column_vecs, columns, active)
        forward_out = lax.psum_scatter(
            forward_terms(blocks, picked), "col", scatter_dimension=0, tiled=True
        ).astype(jnp.bfloat16)
        row_vecs = lax.all_gather(forward_out, "col", axis=0, tiled=True)
        partial_value = adjoint_terms(blocks, columns, active, row_vecs, col_count)
        adjoint_out = lax.psum_scatter(
            partial_value.astype(jnp.bfloat16), "row", scatter_dimension=0, tiled=True
        )
        results.append(forward_out)
        results.append(adjoint_out)
        current = adjoint_out
    return (results[0], results[1], results[2], results[3])


def solution(mesh):
    in_specs = (
        P("row", "col", None, None),
        P("row", "col"),
        P("row", "col"),
        P(("col", "row"), None, None),
    )
    out_specs = (
        P(("row", "col"), None, None),
        P(("col", "row"), None, None),
        P(("row", "col"), None, None),
        P(("col", "row"), None, None),
    )
    return jax.shard_map(body, mesh=mesh, in_specs=in_specs, out_specs=out_specs, check_vma=False)
```

profile of v0, /device:TPU:0, one launch (start us, length us, event | category | flops | bytes accessed | tf_op | source)
XLA Modules:
  0.0 566.4 jit_solution(17264336816287896016)
XLA Ops:
  7.2 0.7 all-gather.3.cloned.1.call-update
  7.9 0.7 compare_select_fusion
  8.8 0.7 fusion.14
  9.6 35.0 %all-gather.3.cloned.1.call-done = bf16[128,32,128]{2,1,0:T(8,128)(2,1)} async-done(((bf16[8,32,128]{2,1,0:T(8,128)(2,1)}), bf16[128,32,128]{2,1,0:T(8,128)(2,1)}) %all-gather.3.cloned.1.call-update) | async-done | bytes 1048592 | tf_op jit(solution)/shard_map/all_gather | solution.py:34
  44.6 4.4 gather_fusion
  49.0 10.9 %fusion.6 = f32[64,32,128]{2,1,0:T(8,128)} fusion(bf16[64,8,128,128]{3,2,1,0:T(8,128)(2,1)} %param.4, bf16[64,8,32,128]{3,2,1,0:T(8,128)(2,1)} %bitcast.32, bf16[64,8]{1,0:T(8,128)(2,1)S(1)} %get-tuple-element.5), kind=kOutput, calls=%fused_computation.12 | convolution fusion | flops 538968064 | bytes 22021120 | tf_op jit(solution)/shard_map/isrc,iskc->ikr/dot_general | solution.py:12
  60.1 71.8 %reduce-scatter.5.cloned.1.call-done = f32[8,32,128]{2,1,0:T(8,128)} async-done(((f32[64,32,128]{2,1,0:T(8,128)}), f32[8,32,128]{2,1,0:T(8,128)}) %reduce-scatter.5.cloned.1.call-update) | async-done | bytes 131088 | tf_op jit(solution)/shard_map/reduce_scatter | solution.py:36
  131.9 0.9 convert_element_type.29
  132.9 34.9 %all_gather.13 = bf16[64,32,128]{2,1,0:T(8,128)(2,1)S(1)} all-gather(bf16[8,32,128]{2,1,0:T(8,128)(2,1)S(1)} %convert_element_type.29), channel_id=1, replica_groups=mesh['row'=16,'col'=8] {'col'}, dimensions={0}, use_global_device_ids=true | all-gather | bytes 589824 | tf_op jit(solution)/shard_map/all_gather | solution.py:39
  167.8 11.3 %broadcast_multiply_fusion.1 = f32[64,32,8,128]{3,1,2,0:T(8,128)} fusion(f32[64,8]{1,0:T(8,128)S(1)} %get-tuple-element.4, bf16[64,8,128,128]{3,2,1,0:T(8,128)(2,1)} %param.4, bf16[64,32,128]{2,1,0:T(8,128)(2,1)S(1)} %all_gather.13), kind=kOutput, calls=%fused_computation.7 | convolution fusion | flops 538968064 | bytes 25692160 | tf_op jit(solution)/shard_map/isrc,ikr->iskc/dot_general | solution.py:16
  179.1 0.2 broadcast.40.clone
  179.4 44.6 %scatter_fusion = f32[128,32,128]{2,1,0:T(8,128)S(1)} fusion(f32[128,32,128]{2,1,0:T(8,128)S(1)} %broadcast.40.clone, s32[512]{0:T(512)S(1)} %reshape.78, f32[512,32,128]{2,1,0:T(8,128)} %bitcast.30), kind=kCustom, calls=%fused_computation.2 | custom fusion | flops 2097152 | bytes 25167872 | tf_op jit(solution)/shard_map/scatter-add | solution.py:19
  223.9 1.2 convert_element_type.31
  225.2 60.3 %reduce-scatter.7.cloned.1.call-done = bf16[8,32,128]{2,1,0:T(8,128)(2,1)} async-done(((bf16[128,32,128]{2,1,0:T(8,128)(2,1)}), bf16[8,32,128]{2,1,0:T(8,128)(2,1)}) %reduce-scatter.7.cloned.1.call-update) | async-done | bytes 65552 | tf_op jit(solution)/shard_map/reduce_scatter | solution.py:41
  285.5 33.0 %all-gather.5.cloned.1.call-done = bf16[128,32,128]{2,1,0:T(8,128)(2,1)} async-done(((bf16[8,32,128]{2,1,0:T(8,128)(2,1)}), bf16[128,32,128]{2,1,0:T(8,128)(2,1)}) %all-gather.5.cloned.1.call-update) | async-done | bytes 1048592 | tf_op jit(solution)/shard_map/all_gather | solution.py:34
  318.5 4.4 gather_fusion.1
  322.9 10.9 %fusion.9 = f32[64,32,128]{2,1,0:T(8,128)} fusion(bf16[64,8,128,128]{3,2,1,0:T(8,128)(2,1)} %param.4, bf16[64,8,32,128]{3,2,1,0:T(8,128)(2,1)} %bitcast.31, bf16[64,8]{1,0:T(8,128)(2,1)S(1)} %get-tuple-element.5), kind=kOutput, calls=%fused_computation.13 | convolution fusion | flops 538968064 | bytes 22021120 | tf_op jit(solution)/shard_map/isrc,iskc->ikr/dot_general | solution.py:12
  333.9 72.1 %reduce-scatter.9.cloned.1.call-done = f32[8,32,128]{2,1,0:T(8,128)} async-done(((f32[64,32,128]{2,1,0:T(8,128)}), f32[8,32,128]{2,1,0:T(8,128)}) %reduce-scatter.9.cloned.1.call-update) | async-done | bytes 131088 | tf_op jit(solution)/shard_map/reduce_scatter | solution.py:36
  405.9 0.9 convert_element_type.32
  406.9 35.1 %all_gather.15 = bf16[64,32,128]{2,1,0:T(8,128)(2,1)S(1)} all-gather(bf16[8,32,128]{2,1,0:T(8,128)(2,1)S(1)} %convert_element_type.32), channel_id=1, replica_groups=mesh['row'=16,'col'=8] {'col'}, dimensions={0}, use_global_device_ids=true | all-gather | bytes 589824 | tf_op jit(solution)/shard_map/all_gather | solution.py:39
  441.9 11.3 %broadcast_multiply_fusion = f32[64,32,8,128]{3,1,2,0:T(8,128)} fusion(f32[64,8]{1,0:T(8,128)S(1)} %get-tuple-element.4, bf16[64,8,128,128]{3,2,1,0:T(8,128)(2,1)} %param.4, bf16[64,32,128]{2,1,0:T(8,128)(2,1)S(1)} %all_gather.15), kind=kOutput, calls=%fused_computation.6 | convolution fusion | flops 538968064 | bytes 25692160 | tf_op jit(solution)/shard_map/isrc,ikr->iskc/dot_general | solution.py:16
  453.5 44.6 %scatter_fusion.1 = f32[128,32,128]{2,1,0:T(8,128)S(1)} fusion(f32[128,32,128]{2,1,0:T(8,128)S(1)} %broadcast.40, s32[512]{0:T(512)S(1)} %reshape.78, f32[512,32,128]{2,1,0:T(8,128)} %bitcast.29), kind=kCustom, calls=%fused_computation.3 | custom fusion | flops 2097152 | bytes 25167872 | tf_op jit(solution)/shard_map/scatter-add | solution.py:19
  498.1 1.2 convert_element_type.33
  499.3 60.2 %reduce-scatter.11.cloned.1.call-done = bf16[8,32,128]{2,1,0:T(8,128)(2,1)} async-done(((bf16[128,32,128]{2,1,0:T(8,128)(2,1)}), bf16[8,32,128]{2,1,0:T(8,128)(2,1)}) %reduce-scatter.11.cloned.1.call-update) | async-done | bytes 65552 | tf_op jit(solution)/shard_map/reduce_scatter | solution.py:41
  (23 shorter events, 1.0 us)
Async XLA Ops:
  7.2 37.4 %all-gather.3.cloned.1.call-start = ((), (), s32[]{:S(2)}) async-start(), calls=%async_computation.4 | async-start | bytes 1114112 | tf_op jit(solution)/shard_map/all_gather | solution.py:34
  7.9 124.0 %reduce-scatter.5.cloned.1.call-start = ((), (), s32[]{:S(2)}) async-start(), calls=%async_computation.5 | async-start | bytes 1179648 | tf_op jit(solution)/shard_map/reduce_scatter | solution.py:36
  49.0 11.0 %copy-start.2 = (s32[64,8]{0,1:T(8,128)S(1)}, s32[64,8]{0,1:T(8,128)}, u32[]{:S(2)}) copy-start(s32[64,8]{0,1:T(8,128)} %param.5) | copy-start | bytes 6148
  59.9 225.6 %reduce-scatter.7.cloned.1.call-start = ((), (), s32[]{:S(2)}) async-start(), calls=%async_computation.6 | async-start | bytes 1114112 | tf_op jit(solution)/shard_map/reduce_scatter | solution.py:41
  132.9 46.2 %copy-start = (bf16[8,32,128]{2,1,0:T(8,128)(2,1)}, bf16[8,32,128]{2,1,0:T(8,128)(2,1)S(1)}, u32[]{:S(2)}) copy-start(bf16[8,32,128]{2,1,0:T(8,128)(2,1)S(1)} %convert_element_type.29) | copy-start | bytes 196612
  225.1 93.4 %all-gather.5.cloned.1.call-start = ((), (), s32[]{:S(2)}) async-start(), calls=%async_computation.7 | async-start | bytes 1114112 | tf_op jit(solution)/shard_map/all_gather | solution.py:34
  285.5 120.5 %reduce-scatter.9.cloned.1.call-start = ((), (), s32[]{:S(2)}) async-start(), calls=%async_computation.8 | async-start | bytes 1179648 | tf_op jit(solution)/shard_map/reduce_scatter | solution.py:36
  333.8 225.7 %reduce-scatter.11.cloned.1.call-start = ((), (), s32[]{:S(2)}) async-start(), calls=%async_computation.9 | async-start | bytes 1114112 | tf_op jit(solution)/shard_map/reduce_scatter | solution.py:41
  406.9 46.4 %copy-start.1 = (bf16[8,32,128]{2,1,0:T(8,128)(2,1)}, bf16[8,32,128]{2,1,0:T(8,128)(2,1)S(1)}, u32[]{:S(2)}) copy-start(bf16[8,32,128]{2,1,0:T(8,128)(2,1)S(1)} %convert_element_type.32) | copy-start | bytes 196612
Sparse Core Ops, SparseCore 0:
  9.7 34.8 all-gather.2
  60.0 71.8 reduce-scatter.4
  225.3 60.1 reduce-scatter.6
  287.6 30.9 all-gather.4
  334.0 71.9 reduce-scatter.8
  499.4 60.0 reduce-scatter.10
where the time goes:
time: 569 us; the launch traced here: 566 us
  waiting for transfers between devices  333 us (59%)
  other arithmetic  94.7 us (17%)
  blocking collectives  70 us (12%)
  matrix products  44.5 us (8%)
  between operations  14.2 us (2%)
  local copies, waits for them, and re-layouts  9.62 us (2%)
    reduce_scatter x2, waiting for transfers between devices, body(): lax.psum_scatter(forward_terms(blocks, picked), 'col', scatter_dimension=...  144 us
    reduce_scatter x2, waiting for transfers between devices, body(): lax.psum_scatter(partial_value.astype(jnp.bfloat16), 'row', scatter_dimen...  120 us
    scatter-add x2, other arithmetic, adjoint_terms(): jax.ops.segment_sum(terms.reshape(slot_total, terms.shape[2], terms.shape...  89.1 us
    all_gather x2, blocking collectives, body(): row_vecs = lax.all_gather(forward_out, 'col', axis=0, tiled=True)  70 us
    all_gather x2, waiting for transfers between devices, body(): column_vecs = lax.all_gather(current, 'row', axis=0, tiled=True)  68.1 us
    dot_general x2, matrix products, adjoint_terms(): jnp.einsum('isrc,ikr->iskc', blocks, row_vecs, preferred_element_type=jnp...  22.7 us
    dot_general x2, matrix products, forward_terms(): jnp.einsum('isrc,iskc->ikr', blocks, picked, preferred_element_type=jnp.f...  21.8 us
  transfers between devices with their start and end apart: 6, of which 6 were waited for; matrix products, arithmetic and copies ran while one was open for 0% of the time, Pallas kernels for 0%

commit v1 on v0

--- a/solution.py
+++ b/solution.py
@@ -2,6 +2,11 @@
 import jax.numpy as jnp
 from jax import lax
 from jax.sharding import PartitionSpec as P
+
+
+def gather_over(block, axis, d):
+    stack = jnp.stack([block] * lax.axis_size(axis))
+    return jnp.concatenate(lax.all_to_all(stack, axis, 0, 0), axis=d)
 
 
 def pick_blocks(column_vecs, columns, active):
@@ -36,7 +41,7 @@
         forward_out = lax.psum_scatter(
             forward_terms(blocks, picked), "col", scatter_dimension=0, tiled=True
         ).astype(jnp.bfloat16)
-        row_vecs = lax.all_gather(forward_out, "col", axis=0, tiled=True)
+        row_vecs = gather_over(forward_out, "col", 0)
         partial_value = adjoint_terms(blocks, columns, active, row_vecs, col_count)
         adjoint_out = lax.psum_scatter(
             partial_value.astype(jnp.bfloat16), "row", scatter_dimension=0, tiled=True

time: 569 us -> 526 us (0.924)
  blocking collectives: 70 us -> 14.5 us
  waiting for transfers between devices: 333 us -> 340 us
    all_gather x2 -> x0, blocking collectives: 70 us -> none  [body(): row_vecs = lax.all_gather(forward_out, 'col', axis=0, tiled=True)]
    all_to_all x0 -> x1, blocking collectives: none -> 14.5 us  [gather_over(): return jnp.concatenate(lax.all_to_all(stack, axis, 0, 0), axis=d)]
    all_to_all x0 -> x1, waiting for transfers between devices: none -> 9.55 us  [gather_over(): return jnp.concatenate(lax.all_to_all(stack, axis, 0, 0), axis=d)]
  transfers between devices with their start and end apart: 6 -> 7, of which waited for: 6 -> 7; matrix products, arithmetic and copies ran while one was open for 0% -> 0% of each run, Pallas kernels for 0% -> 0%
where the time goes in v1:
time: 526 us; the launch traced here: 524 us
  waiting for transfers between devices  340 us (65%)
  other arithmetic  94.8 us (18%)
  matrix products  44.5 us (8%)
  blocking collectives  14.5 us (3%)
  between operations  14.2 us (3%)
  local copies, waits for them, and re-layouts  10.6 us (2%)
    reduce_scatter x2, waiting for transfers between devices, body(): lax.psum_scatter(forward_terms(blocks, picked), 'col', scatter_dimension=...  144 us
    reduce_scatter x2, waiting for transfers between devices, body(): lax.psum_scatter(partial_value.astype(jnp.bfloat16), 'row', scatter_dimen...  118 us
    scatter-add x2, other arithmetic, adjoint_terms(): jax.ops.segment_sum(terms.reshape(slot_total, terms.shape[2], terms.shape...  89.1 us
    all_gather x2, waiting for transfers between devices, body(): column_vecs = lax.all_gather(current, 'row', axis=0, tiled=True)  68.3 us
    dot_general x2, matrix products, adjoint_terms(): jnp.einsum('isrc,ikr->iskc', blocks, row_vecs, preferred_element_type=jnp...  22.7 us
    dot_general x2, matrix products, forward_terms(): jnp.einsum('isrc,iskc->ikr', blocks, picked, preferred_element_type=jnp.f...  21.8 us
    all_to_all x1, blocking collectives, gather_over(): return jnp.concatenate(lax.all_to_all(stack, axis, 0, 0), axis=d)  14.5 us
  transfers between devices with their start and end apart: 7, of which 7 were waited for; matrix products, arithmetic and copies ran while one was open for 0% of the time, Pallas kernels for 0%

profile of v1, /device:TPU:0, one launch (start us, length us, event | category | flops | bytes accessed | tf_op | source)
XLA Modules:
  0.0 523.7 jit_solution(11639336517730831018)
XLA Ops:
  7.9 0.7 compare_select_fusion
  8.8 0.7 fusion.12
  9.6 35.0 %all-gather.3.cloned.1.call-done = bf16[128,32,128]{2,1,0:T(8,128)(2,1)} async-done(((bf16[8,32,128]{2,1,0:T(8,128)(2,1)}), bf16[128,32,128]{2,1,0:T(8,128)(2,1)}) %all-gather.3.cloned.1.call-update) | async-done | bytes 1048592 | tf_op jit(solution)/shard_map/all_gather | solution.py:39
  44.6 4.4 gather_fusion
  49.0 10.9 %fusion.6 = f32[64,32,128]{2,1,0:T(8,128)} fusion(bf16[64,8,128,128]{3,2,1,0:T(8,128)(2,1)} %param.4, bf16[64,8,32,128]{3,2,1,0:T(8,128)(2,1)} %bitcast.34, bf16[64,8]{1,0:T(8,128)(2,1)S(1)} %get-tuple-element.5), kind=kOutput, calls=%fused_computation.12 | convolution fusion | flops 538968064 | bytes 22021120 | tf_op jit(solution)/shard_map/isrc,iskc->ikr/dot_general | solution.py:17
  59.9 72.1 %reduce-scatter.5.cloned.1.call-done = f32[8,32,128]{2,1,0:T(8,128)} async-done(((f32[64,32,128]{2,1,0:T(8,128)}), f32[8,32,128]{2,1,0:T(8,128)}) %reduce-scatter.5.cloned.1.call-update) | async-done | bytes 131088 | tf_op jit(solution)/shard_map/reduce_scatter | solution.py:41
  132.0 0.9 convert_element_type.29
  133.0 0.9 stack.4
  133.8 4.5 all-to-all-start
  138.6 9.6 %all-to-all-done = bf16[8,8,32,128]{3,2,1,0:T(8,128)(2,1)S(1)} async-done(((bf16[8,8,32,128]{3,2,1,0:T(8,128)(2,1)}), bf16[8,8,32,128]{3,2,1,0:T(8,128)(2,1)S(1)}, u32[]{:S(2)}, u32[]{:S(2)}) %all-to-all-start) | async-done | bytes 524320 | tf_op jit(solution)/shard_map/all_to_all | solution.py:9
  148.2 11.3 %broadcast_multiply_fusion.1 = f32[64,32,8,128]{3,1,2,0:T(8,128)} fusion(f32[64,8]{1,0:T(8,128)S(1)} %get-tuple-element.4, bf16[64,32,128,1]{2,1,3,0:T(8,128)(2,1)S(1)} %bitcast.35, bf16[64,8,128,128]{3,2,1,0:T(8,128)(2,1)} %param.4), kind=kOutput, calls=%fused_computation.7 | convolution fusion | flops 538968064 | bytes 25692160 | tf_op jit(solution)/shard_map/isrc,ikr->iskc/dot_general | solution.py:21
  159.7 44.6 %scatter_fusion = f32[128,32,128]{2,1,0:T(8,128)S(1)} fusion(f32[128,32,128]{2,1,0:T(8,128)S(1)} %broadcast.44.clone, s32[512]{0:T(512)S(1)} %reshape.90, f32[512,32,128]{2,1,0:T(8,128)} %bitcast.32), kind=kCustom, calls=%fused_computation.2 | custom fusion | flops 2097152 | bytes 25167872 | tf_op jit(solution)/shard_map/scatter-add | solution.py:24
  204.3 1.2 convert_element_type.31
  205.6 58.9 %reduce-scatter.7.cloned.1.call-done = bf16[8,32,128]{2,1,0:T(8,128)(2,1)} async-done(((bf16[128,32,128]{2,1,0:T(8,128)(2,1)}), bf16[8,32,128]{2,1,0:T(8,128)(2,1)}) %reduce-scatter.7.cloned.1.call-update) | async-done | bytes 65552 | tf_op jit(solution)/shard_map/reduce_scatter | solution.py:46
  264.5 33.3 %all-gather.5.cloned.1.call-done = bf16[128,32,128]{2,1,0:T(8,128)(2,1)} async-done(((bf16[8,32,128]{2,1,0:T(8,128)(2,1)}), bf16[128,32,128]{2,1,0:T(8,128)(2,1)}) %all-gather.5.cloned.1.call-update) | async-done | bytes 1048592 | tf_op jit(solution)/shard_map/all_gather | solution.py:39
  297.8 4.4 gather_fusion.1
  302.2 10.9 %fusion.9 = f32[64,32,128]{2,1,0:T(8,128)} fusion(bf16[64,8,128,128]{3,2,1,0:T(8,128)(2,1)} %param.4, bf16[64,8,32,128]{3,2,1,0:T(8,128)(2,1)} %bitcast.33, bf16[64,8]{1,0:T(8,128)(2,1)S(1)} %get-tuple-element.5), kind=kOutput, calls=%fused_computation.13 | convolution fusion | flops 538968064 | bytes 22021120 | tf_op jit(solution)/shard_map/isrc,iskc->ikr/dot_general | solution.py:17
  313.1 72.1 %reduce-scatter.9.cloned.1.call-done = f32[8,32,128]{2,1,0:T(8,128)} async-done(((f32[64,32,128]{2,1,0:T(8,128)}), f32[8,32,128]{2,1,0:T(8,128)}) %reduce-scatter.9.cloned.1.call-update) | async-done | bytes 131088 | tf_op jit(solution)/shard_map/reduce_scatter | solution.py:41
  385.2 0.9 convert_element_type.32
  386.2 14.5 %all_to_all.10 = bf16[8,8,32,128]{3,2,1,0:T(8,128)(2,1)S(1)} all-to-all(bf16[8,8,32,128]{3,2,1,0:T(8,128)(2,1)S(1)} %stack.5), channel_id=1, replica_groups=mesh['row'=16,'col'=8] {'col'}, dimensions={0} | all-to-all | bytes 1048576 | tf_op jit(solution)/shard_map/all_to_all | solution.py:9
  400.7 11.4 %broadcast_multiply_fusion = f32[64,32,8,128]{3,1,2,0:T(8,128)} fusion(f32[64,8]{1,0:T(8,128)S(1)} %get-tuple-element.4, bf16[64,32,128,1]{2,1,3,0:T(8,128)(2,1)S(1)} %bitcast.36, bf16[64,8,128,128]{3,2,1,0:T(8,128)(2,1)} %param.4), kind=kOutput, calls=%fused_computation.6 | convolution fusion | flops 538968064 | bytes 25692160 | tf_op jit(solution)/shard_map/isrc,ikr->iskc/dot_general | solution.py:21
  412.3 44.6 %scatter_fusion.1 = f32[128,32,128]{2,1,0:T(8,128)S(1)} fusion(f32[128,32,128]{2,1,0:T(8,128)S(1)} %broadcast.44, s32[512]{0:T(512)S(1)} %reshape.90, f32[512,32,128]{2,1,0:T(8,128)} %bitcast.31), kind=kCustom, calls=%fused_computation.3 | custom fusion | flops 2097152 | bytes 25167872 | tf_op jit(solution)/shard_map/scatter-add | solution.py:24
  456.9 1.2 convert_element_type.33
  458.1 58.7 %reduce-scatter.11.cloned.1.call-done = bf16[8,32,128]{2,1,0:T(8,128)(2,1)} async-done(((bf16[128,32,128]{2,1,0:T(8,128)(2,1)}), bf16[8,32,128]{2,1,0:T(8,128)(2,1)}) %reduce-scatter.11.cloned.1.call-update) | async-done | bytes 65552 | tf_op jit(solution)/shard_map/reduce_scatter | solution.py:46
  (26 shorter events, 2.0 us)
Async XLA Ops:
  7.2 37.4 %all-gather.3.cloned.1.call-start = ((), (), s32[]{:S(2)}) async-start(), calls=%async_computation.6 | async-start | bytes 1114112 | tf_op jit(solution)/shard_map/all_gather | solution.py:39
  7.9 124.1 %reduce-scatter.5.cloned.1.call-start = ((), (), s32[]{:S(2)}) async-start(), calls=%async_computation.7 | async-start | bytes 1179648 | tf_op jit(solution)/shard_map/reduce_scatter | solution.py:41
  49.0 89.5 %copy-start.2 = (s32[64,8]{0,1:T(8,128)S(1)}, s32[64,8]{0,1:T(8,128)}, u32[]{:S(2)}) copy-start(s32[64,8]{0,1:T(8,128)} %param.5) | copy-start | bytes 6148
  132.9 26.5 %copy-start = (bf16[8,32,128]{2,1,0:T(8,128)(2,1)}, bf16[8,32,128]{2,1,0:T(8,128)(2,1)S(1)}, u32[]{:S(2)}) copy-start(bf16[8,32,128]{2,1,0:T(8,128)(2,1)S(1)} %convert_element_type.29) | copy-start | bytes 196612
  133.8 14.3 %all-to-all-start = ((bf16[8,8,32,128]{3,2,1,0:T(8,128)(2,1)}), bf16[8,8,32,128]{3,2,1,0:T(8,128)(2,1)S(1)}, u32[]{:S(2)}, u32[]{:S(2)}) async-start(bf16[8,8,32,128]{3,2,1,0:T(8,128)(2,1)} %stack.4), calls=%async_computation.1 | async-start | bytes 1048576 | tf_op jit(solution)/shard_map/all_to_all | solution.py:9
  138.4 126.1 %reduce-scatter.7.cloned.1.call-start = ((), (), s32[]{:S(2)}) async-start(), calls=%async_computation.8 | async-start | bytes 1114112 | tf_op jit(solution)/shard_map/reduce_scatter | solution.py:46
  205.5 92.3 %all-gather.5.cloned.1.call-start = ((), (), s32[]{:S(2)}) async-start(), calls=%async_computation.9 | async-start | bytes 1114112 | tf_op jit(solution)/shard_map/all_gather | solution.py:39
  264.5 120.7 %reduce-scatter.9.cloned.1.call-start = ((), (), s32[]{:S(2)}) async-start(), calls=%async_computation.10 | async-start | bytes 1179648 | tf_op jit(solution)/shard_map/reduce_scatter | solution.py:41
  313.1 203.7 %reduce-scatter.11.cloned.1.call-start = ((), (), s32[]{:S(2)}) async-start(), calls=%async_computation.11 | async-start | bytes 1114112 | tf_op jit(solution)/shard_map/reduce_scatter | solution.py:46
  386.1 25.9 %copy-start.1 = (bf16[8,32,128]{2,1,0:T(8,128)(2,1)}, bf16[8,32,128]{2,1,0:T(8,128)(2,1)S(1)}, u32[]{:S(2)}) copy-start(bf16[8,32,128]{2,1,0:T(8,128)(2,1)S(1)} %convert_element_type.32) | copy-start | bytes 196612
Sparse Core Ops, SparseCore 0:
  9.7 34.8 all-gather.2
  60.0 71.9 reduce-scatter.4
  205.6 58.7 reduce-scatter.6
  266.6 31.1 all-gather.4
  313.2 71.9 reduce-scatter.8
  458.2 58.5 reduce-scatter.10
